TPU v7x, 32 devices: a whole 2x2x4 slice. The times are simulated.
32 devices in a mesh: orb: 8 (over y, x, core), probe: 4 (over z).
Axes of the slice: x: 2, y: 2, z: 4, core: 2. Of those that a mesh axis runs over, the one named last changes fastest.
Arguments:
- tiles: bfloat16 [32, 9, 256, 256], P('orb', None, 'probe'), may hold values from -0.0625 to 0.0625
- pattern: int32 [32, 9], P('orb'), may hold values from 0 to 1, as said below
- signs: int32 [8192, 512], P('orb', 'probe'), may hold values from 0 to 1
- previous: bfloat16 [8192, 512], P('orb', 'probe'), may hold values from -6 to 6
- current: bfloat16 [8192, 512], P('orb', 'probe'), may hold values from -6 to 6
Outputs:
- older: bfloat16 [8192, 512], P('orb', 'probe')
- newest: bfloat16 [8192, 512], P('orb', 'probe')
- moments: float32 [4, 512], P(None, 'probe')
Inputs may be any that keep to these rules, and one draw needn't show every extreme that they name: pattern[I, 4] is 1 for every row block; each row block has 4 to 9 ones; the 4 row blocks of one index of orb hold at most 28 ones together, and some index of orb holds exactly 28.
All inputs are finite; a program needn't handle non-finite values.
Results may differ from a plain program's by a relative error of at most 0.0053.
Values may be sent and summed in bfloat16 or wider, within the bound.
A program may use at most 64 MiB of HBM per device.

v0:
```python
import math
import jax
import jax.numpy as jnp
from jax import lax
from jax.sharding import PartitionSpec as P

REACH = 4
STEPS = 4


def extended(array, sides, width):
    for axis, dim in sides:
        peers, length = (lax.axis_size(axis), array.shape[dim])
        up = [(i, (i + 1) % peers) for i in range(peers)]
        down = [(j, i) for i, j in up]
        last = lax.slice_in_dim(array, length - width, length, axis=dim)
        initial = lax.slice_in_dim(array, 0, width, axis=dim)
        before = lax.ppermute(last, axis, up)
        after = lax.ppermute(initial, axis, down)
        array = jnp.concatenate([before, array, after], axis=dim)
    return array


def extend_panel(vec, block_rows):
    return extended(vec, (("orb", 0),), REACH * block_rows)


def body(tiles, pattern, signs, previous, current):
    row_blocks, offsets, shard_rows, block_rows = tiles.shape
    probe_count = previous.shape[1]
    sign_f = (2 * signs - 1).astype(jnp.float32)
    factor = 1.0 / math.sqrt(lax.axis_size("orb") * row_blocks * block_rows)
    full_tiles = lax.all_gather(tiles, "probe", axis=2, tiled=True)
    mask_b = pattern.astype(jnp.bfloat16)
    older, newest = (previous, current)
    collected = []
    for step in range(STEPS):
        blocks = extend_panel(newest, block_rows).reshape(
            row_blocks + 2 * REACH, block_rows, probe_count
        )
        windows = jnp.stack(
            [blocks[offset : offset + row_blocks] for offset in range(offsets)], axis=1
        )
        windows = windows * mask_b[:, :, None, None]
        total = jnp.einsum(
            "roij,rojp->rip", full_tiles, windows, preferred_element_type=jnp.float32
        )
        image = total.reshape(row_blocks * block_rows, probe_count)
        nxt = (2.0 * image - older.astype(jnp.float32)).astype(jnp.bfloat16)
        local_sum = jnp.sum(sign_f * nxt.astype(jnp.float32), axis=0)
        collected.append(lax.psum(local_sum, "orb") * factor)
        older, newest = (newest, nxt)
    stacked = jnp.stack(collected)
    return (older, newest, stacked)


def solution(mesh):
    placed = (
        P("orb", None, "probe", None),
        P("orb", None),
        P("orb", "probe"),
        P("orb", "probe"),
        P("orb", "probe"),
    )
    return jax.shard_map(
        body,
        mesh=mesh,
        in_specs=placed,
        out_specs=(P("orb", "probe"), P("orb", "probe"), P(None, "probe")),
        check_vma=False,
    )
```

profile of v0, /device:TPU:0, one launch (start us, length us, event | category | flops | bytes accessed | tf_op | source)
XLA Modules:
  0.0 224.4 jit_solution(14347151901448904519)
XLA Ops:
  8.4 2.9 %collective-permute-start.1 = (bf16[1024,128]{1,0:T(8,128)(2,1)}, bf16[1024,128]{1,0:T(8,128)(2,1)S(1)}, u32[]{:S(2)}, u32[]{:S(2)}) collective-permute-start(bf16[1024,128]{1,0:T(8,128)(2,1)} %param.9), channel_id=1, source_target_pairs={{4,0},{8,4},{12,8},{16,12},{20,16},{24,20},{28,24},{0,28},{5,1},{9... | collective-permute-start | bytes 786440 | tf_op jit(solution)/shard_map/ppermute | solution.py:19
  11.4 1.1 copy.48
  13.2 2.5 %collective-permute-done = bf16[1024,128]{1,0:T(8,128)(2,1)S(1)} collective-permute-done((bf16[1024,128]{1,0:T(8,128)(2,1)}, bf16[1024,128]{1,0:T(8,128)(2,1)S(1)}, u32[]{:S(2)}, u32[]{:S(2)}) %collective-permute-start) | collective-permute-done | bytes 262176 | tf_op jit(solution)/shard_map/ppermute | solution.py:18
  15.8 1.5 collective-permute-done.1
  20.4 0.9 copy.50
  21.3 0.9 copy.51
  22.1 0.9 copy.52
  23.0 1.1 constant_dynamic-update-slice_fusion.12
  24.1 1.0 constant_dynamic-update-slice_fusion.10
  25.3 76.4 %all-gather.2.cloned.1.call-done = bf16[4,9,256,256]{3,2,1,0:T(8,128)(2,1)} async-done(((bf16[4,9,64,256]{3,2,1,0:T(8,128)(2,1)}), bf16[4,9,256,256]{3,2,1,0:T(8,128)(2,1)}) %all-gather.2.cloned.1.call-update) | async-done | bytes 4718608 | tf_op jit(solution)/shard_map/all_gather | solution.py:33
  101.7 4.0 %fusion.41 = f32[4,256,128]{1,2,0:T(8,128)S(1)} fusion(bf16[4,9,256,256]{3,2,1,0:T(8,128)(2,1)} %all-gather.2.cloned.1.call-done, bf16[4,9,256,128]{2,3,1,0:T(8,128)(2,1)S(1)} %constant_dynamic-update-slice_fusion.4, bf16[4,9]{1,0:T(4,128)(2,1)S(1)} %convert_element_type.38), kind=kOutput, calls=%fused_computation.19 | convolution fusion | flops 605290496 | bytes 7602248 | tf_op jit(solution)/shard_map/roij,rojp->rip/dot_general | solution.py:45
  105.9 1.1 fusion.53
  107.0 2.6 %collective-permute-start.3 = (bf16[1024,128]{1,0:T(8,128)(2,1)S(1)}, bf16[1024,128]{1,0:T(8,128)(2,1)S(1)}, u32[]{:S(2)}, u32[]{:S(2)}) collective-permute-start(bf16[1024,128]{1,0:T(8,128)(2,1)S(1)} %fusion.53), channel_id=1, source_target_pairs={{4,0},{8,4},{12,8},{16,12},{20,16},{24,20},{28,24},{0,28},{5,1},{9... | collective-permute-start | bytes 786440 | tf_op jit(solution)/shard_map/ppermute | solution.py:19
  110.5 4.2 %collective-permute-done.2 = bf16[1024,128]{1,0:T(8,128)(2,1)S(1)} collective-permute-done((bf16[1024,128]{1,0:T(8,128)(2,1)S(1)}, bf16[1024,128]{1,0:T(8,128)(2,1)S(1)}, u32[]{:S(2)}, u32[]{:S(2)}) %collective-permute-start.2) | collective-permute-done | bytes 262176 | tf_op jit(solution)/shard_map/ppermute | solution.py:18
  114.7 1.0 pad_maximum_fusion.4
  115.7 0.9 copy.55
  117.4 1.0 constant_dynamic-update-slice_fusion.21
  118.4 1.8 copy.56
  120.2 1.8 copy.57
  122.0 1.8 copy.59
  123.8 1.8 copy.60
  125.6 0.9 copy.61
  126.6 1.0 constant_dynamic-update-slice_fusion.20
  127.7 1.0 constant_dynamic-update-slice_fusion.19
  128.7 1.0 constant_dynamic-update-slice_fusion.18
  129.6 1.0 constant_dynamic-update-slice_fusion.17
  130.6 1.0 constant_dynamic-update-slice_fusion.16
  131.7 4.0 %fusion.35 = f32[4,256,128]{1,2,0:T(8,128)S(1)} fusion(bf16[4,9,256,256]{3,2,1,0:T(8,128)(2,1)} %all-gather.2.cloned.1.call-done, bf16[4,9,256,128]{2,3,1,0:T(8,128)(2,1)S(1)} %constant_dynamic-update-slice_fusion.13, bf16[4,9]{1,0:T(4,128)(2,1)S(1)} %convert_element_type.38), kind=kOutput, calls=%fused_computation.17 | convolution fusion | flops 605290496 | bytes 7602248 | tf_op jit(solution)/shard_map/roij,rojp->rip/dot_general | solution.py:45
  135.9 1.7 collective-permute-start.4
  137.7 1.1 collective-permute-start.5
  139.6 4.7 %collective-permute-done.4 = bf16[1024,128]{1,0:T(8,128)(2,1)S(1)} collective-permute-done((bf16[1024,128]{1,0:T(8,128)(2,1)S(1)}, bf16[1024,128]{1,0:T(8,128)(2,1)S(1)}, u32[]{:S(2)}, u32[]{:S(2)}) %collective-permute-start.4) | collective-permute-done | bytes 262176 | tf_op jit(solution)/shard_map/ppermute | solution.py:18
  144.4 1.0 pad_maximum_fusion.2
  147.1 1.0 constant_dynamic-update-slice_fusion.30
  148.1 1.8 copy.66
  149.9 1.8 copy.67
  151.7 1.8 copy.69
  153.5 1.8 copy.70
  155.3 0.9 copy.71
  156.3 1.0 constant_dynamic-update-slice_fusion.29
  157.3 1.0 constant_dynamic-update-slice_fusion.28
  158.3 1.0 constant_dynamic-update-slice_fusion.27
  159.3 1.0 constant_dynamic-update-slice_fusion.26
  160.2 1.0 constant_dynamic-update-slice_fusion.25
  161.3 4.8 %fusion.29 = f32[4,256,128]{1,2,0:T(8,128)} fusion(bf16[4,9,256,256]{3,2,1,0:T(8,128)(2,1)} %all-gather.2.cloned.1.call-done, bf16[4,9,256,128]{2,3,1,0:T(8,128)(2,1)S(1)} %constant_dynamic-update-slice_fusion.22, bf16[4,9]{1,0:T(4,128)(2,1)S(1)} %convert_element_type.38), kind=kOutput, calls=%fused_computation.15 | convolution fusion | flops 605290496 | bytes 7602248 | tf_op jit(solution)/shard_map/roij,rojp->rip/dot_general | solution.py:45
  166.1 1.2 copy.73
  167.5 2.0 collective-permute-start.6
  171.0 5.2 %collective-permute-done.6 = bf16[1024,128]{1,0:T(8,128)(2,1)S(1)} collective-permute-done((bf16[1024,128]{1,0:T(8,128)(2,1)S(1)}, bf16[1024,128]{1,0:T(8,128)(2,1)S(1)}, u32[]{:S(2)}, u32[]{:S(2)}) %collective-permute-start.6) | collective-permute-done | bytes 262176 | tf_op jit(solution)/shard_map/ppermute | solution.py:18
  176.2 1.2 pad_maximum_fusion
  179.0 1.0 constant_dynamic-update-slice_fusion.39
  180.0 1.8 copy.76
  181.8 1.8 copy.77
  183.6 1.8 copy.79
  185.4 1.8 copy.80
  187.2 1.8 copy.81
  189.0 0.9 copy.82
  189.9 1.0 constant_dynamic-update-slice_fusion.38
  190.9 1.0 constant_dynamic-update-slice_fusion.37
  191.9 1.0 constant_dynamic-update-slice_fusion.36
  192.9 1.0 constant_dynamic-update-slice_fusion.35
  193.8 1.0 constant_dynamic-update-slice_fusion.34
  194.9 4.8 %fusion.23 = f32[4,256,128]{1,2,0:T(8,128)} fusion(bf16[4,9,256,256]{3,2,1,0:T(8,128)(2,1)} %all-gather.2.cloned.1.call-done, bf16[4,9,256,128]{2,3,1,0:T(8,128)(2,1)S(1)} %constant_dynamic-update-slice_fusion.31, bf16[4,9]{1,0:T(4,128)(2,1)S(1)} %convert_element_type.38), kind=kOutput, calls=%fused_computation.13 | convolution fusion | flops 605290496 | bytes 7602248 | tf_op jit(solution)/shard_map/roij,rojp->rip/dot_general | solution.py:45
  199.7 1.2 copy.83
  201.0 2.0 fusion.49
  203.0 13.9 %all-reduce = (f32[128]{0:T(128)S(1)}, f32[128]{0:T(128)S(1)}, f32[128]{0:T(128)S(1)}, f32[128]{0:T(128)S(1)}) all-reduce(f32[128]{0:T(128)S(1)} %get-tuple-element.4, f32[128]{0:T(128)S(1)} %get-tuple-element.5, f32[128]{0:T(128)S(1)} %get-tuple-element.6, f32[128]{0:T(128)S(1)} %get-tuple-element.3), channel_id=1, replica_groups=mesh['orb'=8,'probe'=4] {'orb'}, use_global_device_ids=true, to_apply=%region_7.0 | all-reduce | flops 512 | bytes 4096 | tf_op jit(solution)/shard_map/psum | solution.py:51
  (79 shorter events, 14.3 us)
Async XLA Ops:
  7.2 8.6 %copy-start.1 = (bf16[1024,128]{1,0:T(8,128)(2,1)S(1)}, bf16[1024,128]{1,0:T(8,128)(2,1)}, u32[]{:S(2)}) copy-start(bf16[1024,128]{1,0:T(8,128)(2,1)} %param.9) | copy-start | bytes 786436
  7.2 94.5 %all-gather.2.cloned.1.call-start = ((), (), s32[]{:S(2)}) async-start(), calls=%async_computation | async-start | bytes 5898240 | tf_op jit(solution)/shard_map/all_gather | solution.py:33
  7.9 7.8 %collective-permute-start = (bf16[1024,128]{1,0:T(8,128)(2,1)}, bf16[1024,128]{1,0:T(8,128)(2,1)S(1)}, u32[]{:S(2)}, u32[]{:S(2)}) collective-permute-start(bf16[1024,128]{1,0:T(8,128)(2,1)} %param.9), channel_id=1, source_target_pairs={{0,4},{4,8},{8,12},{12,16},{16,20},{20,24},{24,28},{28,0},{1,5},{5... | collective-permute-start | bytes 786440 | tf_op jit(solution)/shard_map/ppermute | solution.py:18
  8.4 8.9 %collective-permute-start.1 = (bf16[1024,128]{1,0:T(8,128)(2,1)}, bf16[1024,128]{1,0:T(8,128)(2,1)S(1)}, u32[]{:S(2)}, u32[]{:S(2)}) collective-permute-start(bf16[1024,128]{1,0:T(8,128)(2,1)} %param.9), channel_id=1, source_target_pairs={{4,0},{8,4},{12,8},{16,12},{20,16},{24,20},{28,24},{0,28},{5,1},{9... | collective-permute-start | bytes 786440 | tf_op jit(solution)/shard_map/ppermute | solution.py:19
  23.0 2.1 copy-start.5
  23.0 2.2 copy-start.3
  23.0 2.2 copy-start.4
  23.0 2.2 copy-start.2
  107.0 7.7 %collective-permute-start.2 = (bf16[1024,128]{1,0:T(8,128)(2,1)S(1)}, bf16[1024,128]{1,0:T(8,128)(2,1)S(1)}, u32[]{:S(2)}, u32[]{:S(2)}) collective-permute-start(bf16[1024,128]{1,0:T(8,128)(2,1)S(1)} %fusion.53), channel_id=1, source_target_pairs={{0,4},{4,8},{8,12},{12,16},{16,20},{20,24},{24,28},{28,0},{1,5},{5... | collective-permute-start | bytes 786440 | tf_op jit(solution)/shard_map/ppermute | solution.py:18
  107.0 7.7 %collective-permute-start.3 = (bf16[1024,128]{1,0:T(8,128)(2,1)S(1)}, bf16[1024,128]{1,0:T(8,128)(2,1)S(1)}, u32[]{:S(2)}, u32[]{:S(2)}) collective-permute-start(bf16[1024,128]{1,0:T(8,128)(2,1)S(1)} %fusion.53), channel_id=1, source_target_pairs={{4,0},{8,4},{12,8},{16,12},{20,16},{24,20},{28,24},{0,28},{5,1},{9... | collective-permute-start | bytes 786440 | tf_op jit(solution)/shard_map/ppermute | solution.py:19
  126.6 4.9 %copy-start.7 = (bf16[4,1,256,128]{2,3,1,0:T(8,128)(2,1)S(1)}, bf16[4,1,256,128]{2,3,1,0:T(8,128)(2,1)}, u32[]{:S(2)}) copy-start(bf16[4,1,256,128]{2,3,1,0:T(8,128)(2,1)} %copy.60) | copy-start | bytes 786436
  126.6 5.0 %copy-start.8 = (bf16[4,1,256,128]{2,3,1,0:T(8,128)(2,1)S(1)}, bf16[4,1,256,128]{2,3,1,0:T(8,128)(2,1)}, u32[]{:S(2)}) copy-start(bf16[4,1,256,128]{2,3,1,0:T(8,128)(2,1)} %copy.61) | copy-start | bytes 786436
  135.9 8.4 %collective-permute-start.4 = (bf16[1024,128]{1,0:T(8,128)(2,1)S(1)}, bf16[1024,128]{1,0:T(8,128)(2,1)S(1)}, u32[]{:S(2)}, u32[]{:S(2)}) collective-permute-start(bf16[1024,128]{1,0:T(8,128)(2,1)S(1)} %fusion.52), channel_id=1, source_target_pairs={{0,4},{4,8},{8,12},{12,16},{16,20},{20,24},{24,28},{28,0},{1,5},{5... | collective-permute-start | bytes 786440 | tf_op jit(solution)/shard_map/ppermute | solution.py:18
  137.7 6.7 %collective-permute-start.5 = (bf16[1024,128]{1,0:T(8,128)(2,1)S(1)}, bf16[1024,128]{1,0:T(8,128)(2,1)S(1)}, u32[]{:S(2)}, u32[]{:S(2)}) collective-permute-start(bf16[1024,128]{1,0:T(8,128)(2,1)S(1)} %fusion.52), channel_id=1, source_target_pairs={{4,0},{8,4},{12,8},{16,12},{20,16},{24,20},{28,24},{0,28},{5,1},{9... | collective-permute-start | bytes 786440 | tf_op jit(solution)/shard_map/ppermute | solution.py:19
  156.3 4.9 %copy-start.9 = (bf16[4,1,256,128]{2,3,1,0:T(8,128)(2,1)S(1)}, bf16[4,1,256,128]{2,3,1,0:T(8,128)(2,1)}, u32[]{:S(2)}) copy-start(bf16[4,1,256,128]{2,3,1,0:T(8,128)(2,1)} %copy.70) | copy-start | bytes 786436
  156.3 5.0 %copy-start.10 = (bf16[4,1,256,128]{2,3,1,0:T(8,128)(2,1)S(1)}, bf16[4,1,256,128]{2,3,1,0:T(8,128)(2,1)}, u32[]{:S(2)}) copy-start(bf16[4,1,256,128]{2,3,1,0:T(8,128)(2,1)} %copy.71) | copy-start | bytes 786436
  167.4 33.5 %copy-start = (bf16[1024,128]{1,0:T(8,128)(2,1)}, bf16[1024,128]{1,0:T(8,128)(2,1)S(1)}, u32[]{:S(2)}) copy-start(bf16[1024,128]{1,0:T(8,128)(2,1)S(1)} %fusion.48) | copy-start | bytes 786436
  167.5 8.7 %collective-permute-start.6 = (bf16[1024,128]{1,0:T(8,128)(2,1)S(1)}, bf16[1024,128]{1,0:T(8,128)(2,1)S(1)}, u32[]{:S(2)}, u32[]{:S(2)}) collective-permute-start(bf16[1024,128]{1,0:T(8,128)(2,1)S(1)} %fusion.48), channel_id=1, source_target_pairs={{0,4},{4,8},{8,12},{12,16},{16,20},{20,24},{24,28},{28,0},{1,5},{5... | collective-permute-start | bytes 786440 | tf_op jit(solution)/shard_map/ppermute | solution.py:18
  169.5 6.7 %collective-permute-start.7 = (bf16[1024,128]{1,0:T(8,128)(2,1)S(1)}, bf16[1024,128]{1,0:T(8,128)(2,1)S(1)}, u32[]{:S(2)}, u32[]{:S(2)}) collective-permute-start(bf16[1024,128]{1,0:T(8,128)(2,1)S(1)} %fusion.48), channel_id=1, source_target_pairs={{4,0},{8,4},{12,8},{16,12},{20,16},{24,20},{28,24},{0,28},{5,1},{9... | collective-permute-start | bytes 786440 | tf_op jit(solution)/shard_map/ppermute | solution.py:19
  189.9 4.9 %copy-start.11 = (bf16[4,1,256,128]{2,3,1,0:T(8,128)(2,1)S(1)}, bf16[4,1,256,128]{2,3,1,0:T(8,128)(2,1)}, u32[]{:S(2)}) copy-start(bf16[4,1,256,128]{2,3,1,0:T(8,128)(2,1)} %copy.80) | copy-start | bytes 786436
  189.9 5.0 %copy-start.12 = (bf16[4,1,256,128]{2,3,1,0:T(8,128)(2,1)S(1)}, bf16[4,1,256,128]{2,3,1,0:T(8,128)(2,1)}, u32[]{:S(2)}) copy-start(bf16[4,1,256,128]{2,3,1,0:T(8,128)(2,1)} %copy.81) | copy-start | bytes 786436
  189.9 5.0 %copy-start.6 = (bf16[4,1,256,128]{2,3,1,0:T(8,128)(2,1)S(1)}, bf16[4,1,256,128]{2,3,1,0:T(8,128)(2,1)}, u32[]{:S(2)}) copy-start(bf16[4,1,256,128]{2,3,1,0:T(8,128)(2,1)} %copy.82) | copy-start | bytes 786436
Sparse Core Ops, SparseCore 0:
  9.6 92.0 all-gather.1
where the time goes:
time: 226 us; the launch traced here: 224 us
  waiting for transfers between devices  95.2 us (42%)
  local copies, waits for them, and re-layouts  63.6 us (28%)
  matrix products  17.6 us (8%)
  between operations  14.6 us (6%)
  blocking collectives  13.9 us (6%)
  starting transfers between devices  11.7 us (5%)
  other arithmetic  7.73 us (3%)
    all_gather x1, waiting for transfers between devices, body(): full_tiles = lax.all_gather(tiles, 'probe', axis=2, tiled=True)  76.4 us
    another operation x40, local copies, waits for them, and re-layouts, body(): jnp.stack([blocks[offset:offset + row_blocks] for offset in range(offsets...  40.6 us
    unnamed x60, local copies, waits for them, and re-layouts  20 us
    dot_general x4, matrix products, body(): jnp.einsum('roij,rojp->rip', full_tiles, windows, preferred_element_type=...  17.6 us
    ppermute x4, waiting for transfers between devices, extended(): before = lax.ppermute(last, axis, up)  16.6 us
    psum x1, blocking collectives, body(): collected.append(lax.psum(local_sum, 'orb') * factor)  13.9 us
    ppermute x4, starting transfers between devices, extended(): after = lax.ppermute(initial, axis, down)  7.37 us
  transfers between devices with their start and end apart: 9, of which 6 were waited for; matrix products, arithmetic and copies ran while one was open for 5% of the time, Pallas kernels for 0%

commit v1 on v0

--- a/solution.py
+++ b/solution.py
@@ -3,6 +3,7 @@
 import jax.numpy as jnp
 from jax import lax
 from jax.sharding import PartitionSpec as P
+from jax.lax import all_gather
 
 REACH = 4
 STEPS = 4
@@ -48,7 +49,7 @@
         image = total.reshape(row_blocks * block_rows, probe_count)
         nxt = (2.0 * image - older.astype(jnp.float32)).astype(jnp.bfloat16)
         local_sum = jnp.sum(sign_f * nxt.astype(jnp.float32), axis=0)
-        collected.append(lax.psum(local_sum, "orb") * factor)
+        collected.append(jnp.sum(all_gather(local_sum, "orb"), 0) * factor)
         older, newest = (newest, nxt)
     stacked = jnp.stack(collected)
     return (older, newest, stacked)

time: 226 us -> 247 us (1.093)
  blocking collectives: 13.9 us -> 35.1 us
    all_gather x0 -> x4, blocking collectives: none -> 35.1 us  [body(): collected.append(jnp.sum(all_gather(local_sum, 'orb'), 0) * factor)]
    psum x1 -> x0, blocking collectives: 13.9 us -> none  [body(): collected.append(lax.psum(local_sum, 'orb') * factor)]
where the time goes in v1:
time: 247 us; the launch traced here: 245 us
  waiting for transfers between devices  95.2 us (39%)
  local copies, waits for them, and re-layouts  63.4 us (26%)
  blocking collectives  35.1 us (14%)
  matrix products  17.6 us (7%)
  between operations  14.5 us (6%)
  starting transfers between devices  11.7 us (5%)
  other arithmetic  7.78 us (3%)
    all_gather x1, waiting for transfers between devices, body(): full_tiles = lax.all_gather(tiles, 'probe', axis=2, tiled=True)  76.5 us
    another operation x40, local copies, waits for them, and re-layouts, body(): jnp.stack([blocks[offset:offset + row_blocks] for offset in range(offsets...  40.4 us
    all_gather x4, blocking collectives, body(): collected.append(jnp.sum(all_gather(local_sum, 'orb'), 0) * factor)  35.1 us
    unnamed x60, local copies, waits for them, and re-layouts  20 us
    dot_general x4, matrix products, body(): jnp.einsum('roij,rojp->rip', full_tiles, windows, preferred_element_type=...  17.6 us
    ppermute x4, waiting for transfers between devices, extended(): before = lax.ppermute(last, axis, up)  16.5 us
    ppermute x4, starting transfers between devices, extended(): after = lax.ppermute(initial, axis, down)  7.37 us
  transfers between devices with their start and end apart: 9, of which 6 were waited for; matrix products, arithmetic and copies ran while one was open for 5% of the time, Pallas kernels for 0%

profile of v1, /device:TPU:0, one launch (start us, length us, event | category | flops | bytes accessed | tf_op | source)
XLA Modules:
  0.0 245.3 jit_solution(14478912724140268293)
XLA Ops:
  8.4 2.9 %collective-permute-start.1 = (bf16[1024,128]{1,0:T(8,128)(2,1)}, bf16[1024,128]{1,0:T(8,128)(2,1)S(1)}, u32[]{:S(2)}, u32[]{:S(2)}) collective-permute-start(bf16[1024,128]{1,0:T(8,128)(2,1)} %param.9), channel_id=1, source_target_pairs={{4,0},{8,4},{12,8},{16,12},{20,16},{24,20},{28,24},{0,28},{5,1},{9... | collective-permute-start | bytes 786440 | tf_op jit(solution)/shard_map/ppermute | solution.py:20
  11.4 1.1 copy.88
  13.2 2.5 %collective-permute-done = bf16[1024,128]{1,0:T(8,128)(2,1)S(1)} collective-permute-done((bf16[1024,128]{1,0:T(8,128)(2,1)}, bf16[1024,128]{1,0:T(8,128)(2,1)S(1)}, u32[]{:S(2)}, u32[]{:S(2)}) %collective-permute-start) | collective-permute-done | bytes 262176 | tf_op jit(solution)/shard_map/ppermute | solution.py:19
  15.8 1.5 collective-permute-done.1
  19.6 0.9 copy.89
  23.0 1.1 constant_dynamic-update-slice_fusion.12
  24.1 1.0 constant_dynamic-update-slice_fusion.10
  25.3 76.5 %all-gather.10.cloned.1.call-done = bf16[4,9,256,256]{3,2,1,0:T(8,128)(2,1)} async-done(((bf16[4,9,64,256]{3,2,1,0:T(8,128)(2,1)}), bf16[4,9,256,256]{3,2,1,0:T(8,128)(2,1)}) %all-gather.10.cloned.1.call-update) | async-done | bytes 4718608 | tf_op jit(solution)/shard_map/all_gather | solution.py:34
  101.7 4.0 %fusion.41 = f32[4,256,128]{1,2,0:T(8,128)S(1)} fusion(bf16[4,9,256,256]{3,2,1,0:T(8,128)(2,1)} %all-gather.10.cloned.1.call-done, bf16[4,9,256,128]{2,3,1,0:T(8,128)(2,1)S(1)} %constant_dynamic-update-slice_fusion.4, bf16[4,9]{1,0:T(4,128)(2,1)S(1)} %convert_element_type.38), kind=kOutput, calls=%fused_computation.19 | convolution fusion | flops 605290496 | bytes 7602248 | tf_op jit(solution)/shard_map/roij,rojp->rip/dot_general | solution.py:46
  105.9 1.1 fusion.53
  107.0 2.6 %collective-permute-start.3 = (bf16[1024,128]{1,0:T(8,128)(2,1)S(1)}, bf16[1024,128]{1,0:T(8,128)(2,1)S(1)}, u32[]{:S(2)}, u32[]{:S(2)}) collective-permute-start(bf16[1024,128]{1,0:T(8,128)(2,1)S(1)} %fusion.53), channel_id=1, source_target_pairs={{4,0},{8,4},{12,8},{16,12},{20,16},{24,20},{28,24},{0,28},{5,1},{9... | collective-permute-start | bytes 786440 | tf_op jit(solution)/shard_map/ppermute | solution.py:20
  109.7 0.9 copy.98
  110.6 4.1 %collective-permute-done.2 = bf16[1024,128]{1,0:T(8,128)(2,1)S(1)} collective-permute-done((bf16[1024,128]{1,0:T(8,128)(2,1)S(1)}, bf16[1024,128]{1,0:T(8,128)(2,1)S(1)}, u32[]{:S(2)}, u32[]{:S(2)}) %collective-permute-start.2) | collective-permute-done | bytes 262176 | tf_op jit(solution)/shard_map/ppermute | solution.py:19
  114.7 1.0 pad_maximum_fusion.4
  117.4 1.0 constant_dynamic-update-slice_fusion.21
  118.4 1.8 copy.96
  120.2 1.8 copy.97
  122.0 1.8 copy.99
  123.7 1.8 copy.100
  126.6 1.0 constant_dynamic-update-slice_fusion.20
  127.6 1.0 constant_dynamic-update-slice_fusion.19
  128.6 1.0 constant_dynamic-update-slice_fusion.18
  129.5 1.0 constant_dynamic-update-slice_fusion.17
  130.5 1.0 constant_dynamic-update-slice_fusion.16
  131.6 4.0 %fusion.35 = f32[4,256,128]{1,2,0:T(8,128)S(1)} fusion(bf16[4,9,256,256]{3,2,1,0:T(8,128)(2,1)} %all-gather.10.cloned.1.call-done, bf16[4,9,256,128]{2,3,1,0:T(8,128)(2,1)S(1)} %constant_dynamic-update-slice_fusion.13, bf16[4,9]{1,0:T(4,128)(2,1)S(1)} %convert_element_type.38), kind=kOutput, calls=%fused_computation.17 | convolution fusion | flops 605290496 | bytes 7602248 | tf_op jit(solution)/shard_map/roij,rojp->rip/dot_general | solution.py:46
  135.8 1.7 collective-permute-start.4
  137.6 1.1 collective-permute-start.5
  138.7 0.9 copy.108
  139.6 4.7 %collective-permute-done.4 = bf16[1024,128]{1,0:T(8,128)(2,1)S(1)} collective-permute-done((bf16[1024,128]{1,0:T(8,128)(2,1)S(1)}, bf16[1024,128]{1,0:T(8,128)(2,1)S(1)}, u32[]{:S(2)}, u32[]{:S(2)}) %collective-permute-start.4) | collective-permute-done | bytes 262176 | tf_op jit(solution)/shard_map/ppermute | solution.py:19
  144.3 1.0 pad_maximum_fusion.2
  147.0 1.0 constant_dynamic-update-slice_fusion.30
  147.9 1.8 copy.106
  149.7 1.8 copy.107
  151.5 1.8 copy.109
  153.3 1.8 copy.110
  156.1 1.0 constant_dynamic-update-slice_fusion.29
  157.1 1.0 constant_dynamic-update-slice_fusion.28
  158.1 1.0 constant_dynamic-update-slice_fusion.27
  159.1 1.0 constant_dynamic-update-slice_fusion.26
  160.1 1.0 constant_dynamic-update-slice_fusion.25
  161.1 4.8 %fusion.29 = f32[4,256,128]{1,2,0:T(8,128)} fusion(bf16[4,9,256,256]{3,2,1,0:T(8,128)(2,1)} %all-gather.10.cloned.1.call-done, bf16[4,9,256,128]{2,3,1,0:T(8,128)(2,1)S(1)} %constant_dynamic-update-slice_fusion.22, bf16[4,9]{1,0:T(4,128)(2,1)S(1)} %convert_element_type.38), kind=kOutput, calls=%fused_computation.15 | convolution fusion | flops 605290496 | bytes 7602248 | tf_op jit(solution)/shard_map/roij,rojp->rip/dot_general | solution.py:46
  165.9 1.2 copy.113
  167.3 2.0 collective-permute-start.6
  169.9 0.9 copy.118
  170.8 5.1 %collective-permute-done.6 = bf16[1024,128]{1,0:T(8,128)(2,1)S(1)} collective-permute-done((bf16[1024,128]{1,0:T(8,128)(2,1)S(1)}, bf16[1024,128]{1,0:T(8,128)(2,1)S(1)}, u32[]{:S(2)}, u32[]{:S(2)}) %collective-permute-start.6) | collective-permute-done | bytes 262176 | tf_op jit(solution)/shard_map/ppermute | solution.py:19
  175.9 1.2 pad_maximum_fusion
  178.8 1.0 constant_dynamic-update-slice_fusion.39
  179.8 1.8 copy.116
  181.6 1.8 copy.117
  183.3 1.8 copy.119
  185.1 1.8 copy.120
  186.9 1.8 copy.121
  189.5 1.0 constant_dynamic-update-slice_fusion.38
  190.6 1.0 constant_dynamic-update-slice_fusion.37
  191.6 1.0 constant_dynamic-update-slice_fusion.36
  192.5 1.0 constant_dynamic-update-slice_fusion.35
  193.5 1.0 constant_dynamic-update-slice_fusion.34
  194.6 4.8 %fusion.23 = f32[4,256,128]{1,2,0:T(8,128)} fusion(bf16[4,9,256,256]{3,2,1,0:T(8,128)(2,1)} %all-gather.10.cloned.1.call-done, bf16[4,9,256,128]{2,3,1,0:T(8,128)(2,1)S(1)} %constant_dynamic-update-slice_fusion.31, bf16[4,9]{1,0:T(4,128)(2,1)S(1)} %convert_element_type.38), kind=kOutput, calls=%fused_computation.13 | convolution fusion | flops 605290496 | bytes 7602248 | tf_op jit(solution)/shard_map/roij,rojp->rip/dot_general | solution.py:46
  199.4 1.2 copy.123
  200.6 2.0 fusion.49
  202.7 11.1 %all-gather.7 = f32[8,1,128]{2,1,0:T(1,128)S(1)} all-gather(f32[1,1,128]{2,1,0:T(1,128)S(1)} %bitcast.140), channel_id=5, replica_groups=mesh['orb'=8,'probe'=4] {'orb'}, dimensions={0}, use_global_device_ids=true | all-gather | bytes 4608 | tf_op jit(solution)/shard_map/all_gather | solution.py:52
  213.8 7.5 %all-gather.6 = f32[8,1,128]{2,1,0:T(1,128)S(1)} all-gather(f32[1,1,128]{2,1,0:T(1,128)S(1)} %bitcast.139), channel_id=4, replica_groups=mesh['orb'=8,'probe'=4] {'orb'}, dimensions={0}, use_global_device_ids=true | all-gather | bytes 4608 | tf_op jit(solution)/shard_map/all_gather | solution.py:52
  221.3 9.0 %all-gather.5 = f32[8,1,128]{2,1,0:T(1,128)S(1)} all-gather(f32[1,1,128]{2,1,0:T(1,128)S(1)} %bitcast.138), channel_id=3, replica_groups=mesh['orb'=8,'probe'=4] {'orb'}, dimensions={0}, use_global_device_ids=true | all-gather | bytes 4608 | tf_op jit(solution)/shard_map/all_gather | solution.py:52
  230.3 7.5 %all-gather.4 = f32[8,1,128]{2,1,0:T(1,128)S(1)} all-gather(f32[1,1,128]{2,1,0:T(1,128)S(1)} %bitcast.137), channel_id=2, replica_groups=mesh['orb'=8,'probe'=4] {'orb'}, dimensions={0}, use_global_device_ids=true | all-gather | bytes 4608 | tf_op jit(solution)/shard_map/all_gather | solution.py:52
  (86 shorter events, 17.0 us)
Async XLA Ops:
  7.2 8.6 %copy-start.1 = (bf16[1024,128]{1,0:T(8,128)(2,1)S(1)}, bf16[1024,128]{1,0:T(8,128)(2,1)}, u32[]{:S(2)}) copy-start(bf16[1024,128]{1,0:T(8,128)(2,1)} %param.9) | copy-start | bytes 786436
  7.2 94.5 %all-gather.10.cloned.1.call-start = ((), (), s32[]{:S(2)}) async-start(), calls=%async_computation | async-start | bytes 5898240 | tf_op jit(solution)/shard_map/all_gather | solution.py:34
  7.9 7.8 %collective-permute-start = (bf16[1024,128]{1,0:T(8,128)(2,1)}, bf16[1024,128]{1,0:T(8,128)(2,1)S(1)}, u32[]{:S(2)}, u32[]{:S(2)}) collective-permute-start(bf16[1024,128]{1,0:T(8,128)(2,1)} %param.9), channel_id=1, source_target_pairs={{0,4},{4,8},{8,12},{12,16},{16,20},{20,24},{24,28},{28,0},{1,5},{5... | collective-permute-start | bytes 786440 | tf_op jit(solution)/shard_map/ppermute | solution.py:19
  8.4 8.9 %collective-permute-start.1 = (bf16[1024,128]{1,0:T(8,128)(2,1)}, bf16[1024,128]{1,0:T(8,128)(2,1)S(1)}, u32[]{:S(2)}, u32[]{:S(2)}) collective-permute-start(bf16[1024,128]{1,0:T(8,128)(2,1)} %param.9), channel_id=1, source_target_pairs={{4,0},{8,4},{12,8},{16,12},{20,16},{24,20},{28,24},{0,28},{5,1},{9... | collective-permute-start | bytes 786440 | tf_op jit(solution)/shard_map/ppermute | solution.py:20
  23.0 2.1 copy-start.5
  23.0 2.2 copy-start.3
  23.0 2.2 copy-start.4
  23.0 2.2 copy-start.2
  107.0 7.7 %collective-permute-start.2 = (bf16[1024,128]{1,0:T(8,128)(2,1)S(1)}, bf16[1024,128]{1,0:T(8,128)(2,1)S(1)}, u32[]{:S(2)}, u32[]{:S(2)}) collective-permute-start(bf16[1024,128]{1,0:T(8,128)(2,1)S(1)} %fusion.53), channel_id=1, source_target_pairs={{0,4},{4,8},{8,12},{12,16},{16,20},{20,24},{24,28},{28,0},{1,5},{5... | collective-permute-start | bytes 786440 | tf_op jit(solution)/shard_map/ppermute | solution.py:19
  107.0 7.7 %collective-permute-start.3 = (bf16[1024,128]{1,0:T(8,128)(2,1)S(1)}, bf16[1024,128]{1,0:T(8,128)(2,1)S(1)}, u32[]{:S(2)}, u32[]{:S(2)}) collective-permute-start(bf16[1024,128]{1,0:T(8,128)(2,1)S(1)} %fusion.53), channel_id=1, source_target_pairs={{4,0},{8,4},{12,8},{16,12},{20,16},{24,20},{28,24},{0,28},{5,1},{9... | collective-permute-start | bytes 786440 | tf_op jit(solution)/shard_map/ppermute | solution.py:20
  126.5 4.9 %copy-start.7 = (bf16[4,1,256,128]{2,3,1,0:T(8,128)(2,1)S(1)}, bf16[4,1,256,128]{2,3,1,0:T(8,128)(2,1)}, u32[]{:S(2)}) copy-start(bf16[4,1,256,128]{2,3,1,0:T(8,128)(2,1)} %copy.100) | copy-start | bytes 786436
  126.5 5.0 %copy-start.8 = (bf16[4,1,256,128]{2,3,1,0:T(8,128)(2,1)S(1)}, bf16[4,1,256,128]{2,3,1,0:T(8,128)(2,1)}, u32[]{:S(2)}) copy-start(bf16[4,1,256,128]{2,3,1,0:T(8,128)(2,1)} %copy.101) | copy-start | bytes 786436
  135.8 8.4 %collective-permute-start.4 = (bf16[1024,128]{1,0:T(8,128)(2,1)S(1)}, bf16[1024,128]{1,0:T(8,128)(2,1)S(1)}, u32[]{:S(2)}, u32[]{:S(2)}) collective-permute-start(bf16[1024,128]{1,0:T(8,128)(2,1)S(1)} %fusion.52), channel_id=1, source_target_pairs={{0,4},{4,8},{8,12},{12,16},{16,20},{20,24},{24,28},{28,0},{1,5},{5... | collective-permute-start | bytes 786440 | tf_op jit(solution)/shard_map/ppermute | solution.py:19
  137.6 6.7 %collective-permute-start.5 = (bf16[1024,128]{1,0:T(8,128)(2,1)S(1)}, bf16[1024,128]{1,0:T(8,128)(2,1)S(1)}, u32[]{:S(2)}, u32[]{:S(2)}) collective-permute-start(bf16[1024,128]{1,0:T(8,128)(2,1)S(1)} %fusion.52), channel_id=1, source_target_pairs={{4,0},{8,4},{12,8},{16,12},{20,16},{24,20},{28,24},{0,28},{5,1},{9... | collective-permute-start | bytes 786440 | tf_op jit(solution)/shard_map/ppermute | solution.py:20
  156.1 4.9 %copy-start.9 = (bf16[4,1,256,128]{2,3,1,0:T(8,128)(2,1)S(1)}, bf16[4,1,256,128]{2,3,1,0:T(8,128)(2,1)}, u32[]{:S(2)}) copy-start(bf16[4,1,256,128]{2,3,1,0:T(8,128)(2,1)} %copy.110) | copy-start | bytes 786436
  156.1 5.0 %copy-start.10 = (bf16[4,1,256,128]{2,3,1,0:T(8,128)(2,1)S(1)}, bf16[4,1,256,128]{2,3,1,0:T(8,128)(2,1)}, u32[]{:S(2)}) copy-start(bf16[4,1,256,128]{2,3,1,0:T(8,128)(2,1)} %copy.111) | copy-start | bytes 786436
  167.2 33.4 %copy-start = (bf16[1024,128]{1,0:T(8,128)(2,1)}, bf16[1024,128]{1,0:T(8,128)(2,1)S(1)}, u32[]{:S(2)}) copy-start(bf16[1024,128]{1,0:T(8,128)(2,1)S(1)} %fusion.48) | copy-start | bytes 786436
  167.3 8.7 %collective-permute-start.6 = (bf16[1024,128]{1,0:T(8,128)(2,1)S(1)}, bf16[1024,128]{1,0:T(8,128)(2,1)S(1)}, u32[]{:S(2)}, u32[]{:S(2)}) collective-permute-start(bf16[1024,128]{1,0:T(8,128)(2,1)S(1)} %fusion.48), channel_id=1, source_target_pairs={{0,4},{4,8},{8,12},{12,16},{16,20},{20,24},{24,28},{28,0},{1,5},{5... | collective-permute-start | bytes 786440 | tf_op jit(solution)/shard_map/ppermute | solution.py:19
  169.3 6.7 %collective-permute-start.7 = (bf16[1024,128]{1,0:T(8,128)(2,1)S(1)}, bf16[1024,128]{1,0:T(8,128)(2,1)S(1)}, u32[]{:S(2)}, u32[]{:S(2)}) collective-permute-start(bf16[1024,128]{1,0:T(8,128)(2,1)S(1)} %fusion.48), channel_id=1, source_target_pairs={{4,0},{8,4},{12,8},{16,12},{20,16},{24,20},{28,24},{0,28},{5,1},{9... | collective-permute-start | bytes 786440 | tf_op jit(solution)/shard_map/ppermute | solution.py:20
  189.5 4.9 %copy-start.11 = (bf16[4,1,256,128]{2,3,1,0:T(8,128)(2,1)S(1)}, bf16[4,1,256,128]{2,3,1,0:T(8,128)(2,1)}, u32[]{:S(2)}) copy-start(bf16[4,1,256,128]{2,3,1,0:T(8,128)(2,1)} %copy.120) | copy-start | bytes 786436
  189.5 5.0 %copy-start.12 = (bf16[4,1,256,128]{2,3,1,0:T(8,128)(2,1)S(1)}, bf16[4,1,256,128]{2,3,1,0:T(8,128)(2,1)}, u32[]{:S(2)}) copy-start(bf16[4,1,256,128]{2,3,1,0:T(8,128)(2,1)} %copy.121) | copy-start | bytes 786436
  189.5 5.0 %copy-start.6 = (bf16[4,1,256,128]{2,3,1,0:T(8,128)(2,1)S(1)}, bf16[4,1,256,128]{2,3,1,0:T(8,128)(2,1)}, u32[]{:S(2)}) copy-start(bf16[4,1,256,128]{2,3,1,0:T(8,128)(2,1)} %copy.122) | copy-start | bytes 786436
Sparse Core Ops, SparseCore 0:
  9.6 92.0 all-gather.9
